TPU v7x, 128 devices: a whole 4x4x4 slice. The times are simulated.
128 devices in a mesh: section: 4 (over z_lo, core), dp: 32 (over x, z_hi, y).
Axes of the slice: x: 4, y: 4, z: 4 (z_hi: 2, z_lo: 2; z = z_hi * 2 + z_lo), core: 2. Of those that a mesh axis runs over, the one named last changes fastest.
Arguments:
- inputs: bfloat16 [2, 64, 64, 6656], P(None, 'dp'), may hold values from -6 to 6
- cotangent: bfloat16 [2, 64, 64, 6656], P(None, 'dp'), may hold values from -6 to 6
- stored: bfloat16 [3, 128, 64, 6656], P(None, 'dp'), may hold values from -6 to 6
- sample_ids: int32 [2, 64], P(None, 'dp'), may hold values from 0 to 127, as said below
- act_exp: int32 [3, 2, 64, 64, 52], P(None, None, 'dp'), may hold values from -4 to 0
- grad_exp: int32 [3, 2, 64, 64, 52], P(None, None, 'dp'), may hold values from -7 to -3
- gain: float32 [4, 6656], P('section'), may hold values from 0.1 to 1.9
- down_weight: bfloat16 [4, 6656, 256], P('section'), may hold values from -0.078125 to 0.078125
- up_weight: bfloat16 [4, 6656, 256], P('section'), may hold values from -0.375 to 0.375
Outputs:
- grad_gain: float32 [4, 6656], P('section')
- grad_down: float32 [4, 6656, 256], P('section', 'dp')
- grad_up: float32 [4, 6656, 256], P('section', 'dp')
Inputs may be any that keep to these rules, and one draw needn't show every extreme that they name: `sample_ids`: for each j, the ids in columns j * 2 to (j + 1) * 2 - 1 of all micro-batches together are the numbers j * 4 to (j + 1) * 4 - 1, each once.
All inputs are finite; a program needn't handle non-finite values.
Results may differ from a plain program's by a relative error of at most 0.015.
Values may be sent and summed in bfloat16 or wider, within the bound.
A program may use at most 320 MiB of HBM per device.

v0:
```python
import functools
import math

import jax
import jax.numpy as jnp
from jax import lax
from jax.experimental import pallas as pl
from jax.experimental.pallas import tpu as pltpu
from jax.sharding import PartitionSpec as P

EPS = 1e-05
MESH = pl.DeviceIdType.MESH
F32 = jnp.float32
BF16 = jnp.bfloat16
C = 32
TW = 512
NX, NZ, NY = 4, 2, 4
BR = 208


def dot_nn(a, b):
    return jnp.dot(a, b, preferred_element_type=F32)


def dot_tn(a, b):
    return lax.dot_general(a, b, (((0,), (0,)), ((), ())), preferred_element_type=F32)


def kernel(
    factor,
    ids_ref, inputs, cotangent, stored, act_exp, grad_exp, gain, down, up,
    out_gain, out_down, out_up,
    x_st, dyb_st, xn_st, xout, dyout, down_v, up_v, stored_v, ascale, gscale,
    act_v, grad_v, gain_v, turn_v, pad_v, r_st, p_st, ybuf, gg, acc_v, up_t, down_t,
    xnq, dybq, dpq, hq, p1_0, p1_1, rel2, frl2, q2, qrecv, gx,
    load_sem, xin_sem, xs_sem, dy_sem, ds_sem, ex_send, ex_recv, rs_send, rs_recv,
    gs_send, gs_recv, z_send, z_recv, q_send, q_recv,
):
    tokens, width = x_st.shape
    nchunk = tokens // C
    seq = inputs.shape[2]
    per = seq // C
    ntile = width // TW
    s = lax.axis_index("section")
    dp = lax.axis_index("dp")
    xc = lax.div(dp, NZ * NY)
    zc = lax.rem(lax.div(dp, NY), NZ)
    yc = lax.rem(dp, NY)
    last = lax.axis_size("section") - 1

    def at_x(t):
        return t * (NZ * NY) + zc * NY + yc

    def at_y(t):
        return xc * (NZ * NY) + zc * NY + t

    by_x = [s != last - 1, lax.rem(s, 2) == 0]
    mine = [jnp.where(by_x[kind], xc, yc) for kind in (0, 1)]
    cross = [jnp.where(by_x[kind], yc, xc) for kind in (0, 1)]

    def ring_id(kind, t):
        return jnp.where(by_x[kind], at_x(t), at_y(t))

    def cross_id(kind, t):
        return jnp.where(by_x[kind], at_y(t), at_x(t))

    def owner(kind, z):
        return mine[kind] * (NZ * NY) + z * NY + cross[kind]

    def turned(z):
        return yc * (NZ * NY) + z * NY + xc

    zmate = xc * (NZ * NY) + (1 - zc) * NY + yc

    loads = [
        pltpu.make_async_copy(act_exp.at[jnp.minimum(s, last - 1)], act_v, load_sem.at[0]),
        pltpu.make_async_copy(gain, gain_v, load_sem.at[1]),
        pltpu.make_async_copy(up.at[0], up_v, load_sem.at[2]),
        pltpu.make_async_copy(down.at[0], down_v, load_sem.at[3]),
        pltpu.make_async_copy(stored.at[jnp.minimum(s, last - 1)], stored_v, load_sem.at[4]),
        pltpu.make_async_copy(grad_exp.at[jnp.maximum(s - 1, 0)], grad_v, load_sem.at[5]),
    ]
    loads[0].start()
    loads[1].start()

    def rows_of(c):
        return pl.ds(pl.multiple_of(c * C, C), C)

    def own_rows(source, stash, sem, first, end):
        for c in range(first, end):
            slot = c // per
            pltpu.make_async_copy(
                source.at[slot // 2, slot % 2, pl.ds((c % per) * C, C)],
                stash.at[pl.ds(c * C, C)],
                sem.at[c],
            ).start()

    @pl.when(s == 0)
    def _():
        own_rows(inputs, x_st, xin_sem, 0, 1)

    for load in loads[2:]:
        load.start()

    @pl.when(s == 0)
    def _():
        own_rows(inputs, x_st, xin_sem, 1, nchunk)

    @pl.when(s == last)
    def _():
        own_rows(cotangent, dyb_st, dy_sem, 0, nchunk)

    barrier = pltpu.get_barrier_semaphore()
    for t in range(1, NX):
        pl.semaphore_signal(
            barrier, inc=1, device_id={"dp": at_x(lax.rem(xc + t, NX))}, device_id_type=MESH
        )
        pl.semaphore_signal(
            barrier, inc=1, device_id={"dp": at_y(lax.rem(yc + t, NY))}, device_id_type=MESH
        )
    pl.semaphore_signal(barrier, inc=1, device_id={"dp": zmate}, device_id_type=MESH)

    @pl.when(xc != yc)
    def _():
        for z in range(NZ):
            pl.semaphore_signal(barrier, inc=1, device_id={"dp": turned(z)}, device_id_type=MESH)

    @pl.when(s > 0)
    def _():
        pl.semaphore_signal(barrier, inc=1, device_id={"section": s - 1}, device_id_type=MESH)

    @pl.when(s < last)
    def _():
        pl.semaphore_signal(barrier, inc=1, device_id={"section": s + 1}, device_id_type=MESH)

    def expand(exps, out, first, count):
        turn_v[...] = jnp.zeros_like(turn_v)
        for m in range(exps.shape[0]):
            for i in range(exps.shape[2]):
                own = exps[m, :, i, :]
                scale = jnp.left_shift(jnp.ones(own.shape, jnp.int32), own + 8).astype(F32) / 256.0
                at = (m * exps.shape[2] + i) * seq
                turn_v[: exps.shape[1], at : at + seq] = scale
        pad_v[...] = jnp.transpose(turn_v[...]).astype(BF16)

        def tile(k, carry):
            cols = pl.ds(pl.multiple_of(k * TW, TW), TW)
            block = lax.broadcasted_iota(jnp.int32, (pad_v.shape[1], TW), 0)
            lane = lax.broadcasted_iota(jnp.int32, (pad_v.shape[1], TW), 1)
            pick = (block == k * (TW // 128) + jnp.right_shift(lane, 7)).astype(F32).astype(BF16)
            some = pl.ds(first, count)
            out[some, cols] = dot_nn(pad_v[some, :], pick).astype(BF16)
            return carry

        lax.fori_loop(0, ntile, tile, 0)

    gg[...] = jnp.zeros_like(gg)
    acc_v[...] = jnp.zeros_like(acc_v)
    def transpose(source, out):
        def tile(k, carry):
            cols = pl.ds(pl.multiple_of(k * TW, TW), TW)
            out[:, cols] = jnp.transpose(source[cols, :])
            return carry

        lax.fori_loop(0, ntile, tile, 0)

    loads[0].wait()

    @pl.when(s == 0)
    def _():
        expand(act_v, ascale, 0, 2 * C)

    @pl.when((s > 0) & (s < last))
    def _():
        expand(act_v, ascale, 0, tokens)

    loads[2].wait()

    @pl.when(s < last)
    def _():
        transpose(up_v, up_t)

    loads[5].wait()

    @pl.when(s > 0)
    def _():
        expand(grad_v, gscale, 0, tokens)

    loads[1].wait()
    loads[3].wait()

    @pl.when(s >= last - 1)
    def _():
        transpose(down_v, down_t)

    npeer = NX - 1 + NY - 1 + 1
    npeer = npeer + jnp.where(xc != yc, NZ, 0)
    pl.semaphore_wait(barrier, npeer + jnp.where(s > 0, 1, 0) + jnp.where(s < last, 1, 0))

    def send_x(c):
        return pltpu.make_async_remote_copy(
            src_ref=xout.at[rows_of(c)], dst_ref=x_st.at[rows_of(c)],
            send_sem=xs_sem.at[c], recv_sem=xin_sem.at[c],
            device_id={"section": s + 1}, device_id_type=MESH,
        )

    def send_dy(c):
        return pltpu.make_async_remote_copy(
            src_ref=dyout.at[rows_of(c)], dst_ref=dyb_st.at[rows_of(c)],
            send_sem=ds_sem.at[c], recv_sem=dy_sem.at[c],
            device_id={"section": s - 1}, device_id_type=MESH,
        )

    quarter = width // 4
    pair = nchunk // 4

    def quarters(kind, t, stash, out, rows, seg):
        other = lax.rem(mine[kind] + t, 4)
        cols = pl.ds(pl.multiple_of(other * quarter, 128), quarter)
        return pltpu.make_async_remote_copy(
            src_ref=stash.at[rows, cols], dst_ref=out.at[mine[kind], rows],
            send_sem=ex_send.at[kind, 0, t], recv_sem=ex_recv.at[kind, 0, seg, mine[kind]],
            device_id={"dp": ring_id(kind, other)}, device_id_type=MESH,
        )

    def units_of(kind, t, out, rows, seg):
        other = lax.rem(mine[kind] + t, 4)
        return pltpu.make_async_remote_copy(
            src_ref=out.at[mine[kind], rows], dst_ref=out.at[mine[kind], rows],
            send_sem=ex_send.at[kind, 1, t], recv_sem=ex_recv.at[kind, 1, seg, mine[kind]],
            device_id={"dp": ring_id(kind, other)}, device_id_type=MESH,
        )

    def own_quarter(kind, stash, out, rows, seg):
        cols = pl.ds(pl.multiple_of(mine[kind] * quarter, 128), quarter)
        return pltpu.make_async_copy(
            stash.at[rows, cols], out.at[mine[kind], rows], ex_recv.at[kind, 0, seg, mine[kind]]
        )

    def exchange(kind, stash, out, c):
        for t in (2, 1, 3):
            quarters(kind, t, stash, out, rows_of(c), lax.div(c, pair)).start()
        own_quarter(kind, stash, out, rows_of(c), lax.div(c, pair)).start()

    def exchange_units(kind, out, c):
        for t in (2, 1, 3):
            units_of(kind, t, out, rows_of(c), lax.div(c, pair)).start()

    def exchanged(kind, part, out, seg):
        rows = pl.ds(pl.multiple_of(seg * (pair * C), pair * C), pair * C)
        for t in range(1 if part else 0, 4):
            other = lax.rem(mine[kind] + t, 4)
            pltpu.make_async_copy(
                out.at[other, rows], out.at[other, rows], ex_recv.at[kind, part, seg, other]
            ).wait()

    def grads(kind, seg):
        data, units = ((xnq, dpq), (dybq, hq))[kind]
        exchanged(kind, 0, data, seg)
        exchanged(kind, 1, units, seg)
        rows = pl.ds(pl.multiple_of(seg * (pair * C), pair * C), pair * C)
        left = data[:, rows, :].reshape(4 * pair * C, quarter)
        right = units[:, rows, :].reshape(4 * pair * C, units.shape[2])
        acc_v[kind] += dot_tn(left, right)

    def cols_of(k):
        return pl.ds(pl.multiple_of(k * TW, TW), TW)

    def forward(c):
        rows = rows_of(c)
        pltpu.make_async_copy(x_st.at[rows], x_st.at[rows], xin_sem.at[c]).wait()

        def project(k, carry):
            squares, total = carry
            cols = cols_of(k)
            x = x_st[rows, cols].astype(F32)
            xg = (x * gain_v[:, cols]).astype(BF16)
            xn_st[rows, cols] = xg
            return squares + x * x, total + dot_nn(xg, down_v[cols, :])

        squares, total = lax.fori_loop(
            0, ntile, project,
            (jnp.zeros((C, TW), F32), jnp.zeros((C, down_v.shape[1]), F32)), unroll=True,
        )
        recip = lax.rsqrt(jnp.sum(squares, axis=1, keepdims=True) / width + EPS)
        r_st[rows, :] = jnp.broadcast_to(recip, (C, 128))
        pre = total * recip
        hidden = (pre * jax.nn.sigmoid(pre)).astype(BF16)
        p_st[rows, :] = pre
        hq[mine[1], rows, :] = hidden

        @pl.when(c == 0)
        def _():
            loads[4].wait()

        @pl.when(s < last)
        def _():
            slot = lax.div(c, per)
            pos = pl.ds(pl.multiple_of(lax.rem(c, per) * C, C), C)
            own = ids_ref[lax.div(slot, 2), lax.rem(slot, 2)] - dp * stored_v.shape[0]
            own = jnp.clip(own, 0, stored_v.shape[0] - 1)

            def code(k, carry):
                cols = cols_of(k)
                y = x_st[rows, cols].astype(F32) + dot_nn(hidden, up_t[:, cols])
                base = stored_v[own, pos, cols].astype(F32)
                scale = ascale[rows, cols].astype(F32)
                step = jnp.clip(y - base, -8.0 * scale, 7.0 * scale)
                xout[rows, cols] = (base + step).astype(BF16)
                return carry

            lax.fori_loop(0, ntile, code, 0, unroll=True)
            send_x(c).start()

        exchange(0, xn_st, xnq, c)
        exchange_units(1, hq, c)

    def backward(c):
        rows = rows_of(c)

        @pl.when(s < last)
        def _():
            pltpu.make_async_copy(dyb_st.at[rows], dyb_st.at[rows], dy_sem.at[c]).wait()

        @pl.when(s == 0)
        def _():
            exchange(1, dyb_st, dybq, c)

        dh = dot_nn(dyb_st[rows, :], up_v[...])
        pre = p_st[rows, :]
        sig = jax.nn.sigmoid(pre)
        dpre = (dh * sig * (1.0 + pre * (1.0 - sig))).astype(BF16)
        dpq[mine[0], rows, :] = (
            dpre.astype(F32) * jnp.concatenate([r_st[rows, :]] * (dpre.shape[1] // 128), axis=1)
        ).astype(BF16)
        exchange_units(0, dpq, c)
        wide = jnp.concatenate([r_st[rows, :]] * (TW // 128), axis=1)

        def first(k, acc):
            cols = cols_of(k)
            dxn = dot_nn(dpre, down_t[:, cols])
            ybuf[:, cols] = dxn
            prod = dxn * (x_st[rows, cols].astype(F32) * wide)
            gg[:, cols] += jnp.sum(prod.reshape(C // 8, 8, TW), axis=0)
            return acc + prod * gain_v[:, cols]

        acc = lax.fori_loop(0, ntile, first, jnp.zeros((C, TW), F32), unroll=True)

        @pl.when(s > 0)
        def _():
            mean = jnp.broadcast_to(jnp.sum(acc, axis=1, keepdims=True) / width, (C, TW)) * wide

            def second(k, carry):
                cols = cols_of(k)
                dz = ybuf[:, cols] * gain_v[:, cols]
                grad = wide * (dz - x_st[rows, cols].astype(F32) * mean) + dyb_st[rows, cols].astype(F32)
                scale = gscale[rows, cols].astype(F32)
                dyout[rows, cols] = jnp.clip(grad, -128.0 * scale, 127.0 * scale).astype(BF16)
                return carry

            lax.fori_loop(0, ntile, second, 0, unroll=True)
            send_dy(c).start()

            @pl.when(s < last)
            def _():
                exchange(1, dyb_st, dybq, c)

    @pl.when(s == last)
    def _():
        def early(c, carry):
            rows = rows_of(c)
            pltpu.make_async_copy(dyb_st.at[rows], dyb_st.at[rows], dy_sem.at[c]).wait()
            exchange(1, dyb_st, dybq, c)
            return carry

        lax.fori_loop(0, nchunk, early, 0)

    lag = jnp.where(s == last, 0, jnp.where(s == last - 1, 2, nchunk))

    def step(t, carry):
        @pl.when((t == 1) & (s == 0))
        def _():
            expand(act_v, ascale, 2 * C, tokens - 2 * C)

        @pl.when(t < nchunk)
        def _():
            forward(t)

        @pl.when((t == lag) & (s < last - 1))
        def _():
            transpose(down_v, down_t)

        done = t - lag

        early = (s < last - 1) & (done > pair) & (done < nchunk)

        @pl.when(early & (lax.rem(done, pair) == pair - 1))
        def _():
            for kind in (0, 1):
                grads(kind, lax.div(done, pair) - 1)

        @pl.when((t >= lag) & (t < lag + nchunk))
        def _():
            backward(t - lag)

        return carry

    lax.fori_loop(0, 2 * nchunk, step, 0)

    def gain_send(phase, t):
        coord, at = ((xc, at_x), (yc, at_y))[phase]
        return pltpu.make_async_remote_copy(
            src_ref=gx.at[phase, coord], dst_ref=gx.at[phase, coord],
            send_sem=gs_send.at[phase, t], recv_sem=gs_recv.at[phase, coord],
            device_id={"dp": at(lax.rem(coord + t, 4))}, device_id_type=MESH,
        )

    def gain_wait(phase):
        coord = (xc, yc)[phase]
        for t in range(1, 4):
            other = lax.rem(coord + t, 4)
            pltpu.make_async_copy(
                gx.at[phase, other], gx.at[phase, other], gs_recv.at[phase, other]
            ).wait()

    def gain_sum(phase):
        return (gx[phase, 0] + gx[phase, 1]) + (gx[phase, 2] + gx[phase, 3])

    def settle(kind, out):
        for a in range(2):
            value = acc_v[kind, :, a * 128 : (a + 1) * 128].astype(BF16)
            out[a] = value.reshape(NZ, NY, BR, 128)

    def ring_sends(kind, chunk, rel, frl):
        coord = cross[kind]
        right, left, opp = lax.rem(coord + 1, 4), lax.rem(coord + 3, 4), lax.rem(coord + 2, 4)

        def copy(i, src, dst, to):
            return pltpu.make_async_remote_copy(
                src_ref=src, dst_ref=dst,
                send_sem=rs_send.at[kind, i], recv_sem=rs_recv.at[kind, i],
                device_id={"dp": cross_id(kind, to)}, device_id_type=MESH,
            )

        return [
            copy(0, chunk(0, opp), rel.at[0], right),
            copy(1, chunk(1, opp), rel.at[1], left),
            copy(2, chunk(1, right), frl.at[0, 1], right),
            copy(3, chunk(0, left), frl.at[1, 0], left),
            copy(4, chunk(0, right), frl.at[0, 0], right),
            copy(5, chunk(1, left), frl.at[1, 1], left),
        ]

    sends = [
        ring_sends(0, lambda a, t: p1_0.at[a, :, t], rel2.at[0], frl2.at[0]),
        ring_sends(1, lambda a, t: p1_1.at[a, :, t], rel2.at[1], frl2.at[1]),
    ]

    def add(*refs):
        total = refs[0][...].astype(F32)
        for ref in refs[1:]:
            total = total + ref[...].astype(F32)
        return total

    def loop(n, body):
        def run(i, carry):
            body(i)
            return carry

        lax.fori_loop(0, n, run, 0)

    rings = ((p1_0, cross[0]), (p1_1, cross[1]))

    def begin(kind):
        grads(kind, 3)
        settle(kind, rings[kind][0])
        for i in range(4):
            sends[kind][i].start()

    def relay(kind):
        buf, coord = rings[kind]
        for a, to in ((0, lax.rem(coord + 1, 4)), (1, lax.rem(coord + 3, 4))):
            sends[kind][a].wait_recv()

            def body(v, a=a, to=to):
                buf[a, v, to] = add(buf.at[a, v, to], rel2.at[kind, a, v]).astype(BF16)

            loop(NZ, body)
            sends[kind][4 + a].start()

    def turn(kind, z):
        return pltpu.make_async_remote_copy(
            src_ref=q2.at[kind, z], dst_ref=qrecv.at[kind, zc],
            send_sem=q_send.at[kind, z], recv_sem=q_recv.at[kind, zc],
            device_id={"dp": owner(kind, z)}, device_id_type=MESH,
        )

    def finish(kind):
        buf, coord = rings[kind]
        for i in range(2, 6):
            sends[kind][i].wait_recv()
        for z in (1 - zc, zc):
            for a in range(2):
                q2[kind, z, a] = add(
                    buf.at[a, z, coord], frl2.at[kind, 0, a, z], frl2.at[kind, 1, a, z]
                ).astype(BF16)

            @pl.when(owner(kind, z) != dp)
            def _():
                turn(kind, z).start()

            @pl.when(owner(kind, z) == dp)
            def _():
                pltpu.make_async_copy(
                    q2.at[kind, z], qrecv.at[kind, zc], q_recv.at[kind, zc]
                ).start()

    @pl.when(s >= last - 1)
    def _():
        for kind in (0, 1):
            loop(3, functools.partial(grads, kind))

    nrow = width // 128
    for b in range(nrow):
        gx[0, xc, b : b + 1, :] = jnp.sum(gg[:, b * 128 : (b + 1) * 128], axis=0, keepdims=True)
    for t in range(1, 4):
        gain_send(0, t).start()
    begin(0)
    begin(1)
    gain_wait(0)
    gx[1, yc] = gain_sum(0)
    for t in range(1, 4):
        gain_send(1, t).start()

    relay(0)
    relay(1)
    gain_wait(1)
    gx[2, zc] = gain_sum(1)
    zgain = pltpu.make_async_remote_copy(
        src_ref=gx.at[2, zc], dst_ref=gx.at[2, zc], send_sem=z_send.at[0], recv_sem=z_recv.at[0],
        device_id={"dp": zmate}, device_id_type=MESH,
    )
    zgain.start()
    finish(0)
    finish(1)
    for kind, out in ((0, out_down), (1, out_up)):
        for z in range(NZ):
            pltpu.make_async_copy(
                qrecv.at[kind, z], qrecv.at[kind, z], q_recv.at[kind, z]
            ).wait()
        for a in range(2):
            out[:, a * 128 : (a + 1) * 128] = (
                add(qrecv.at[kind, 0, a], qrecv.at[kind, 1, a]) * factor
            )
    pltpu.make_async_copy(gx.at[2, 1 - zc], gx.at[2, 1 - zc], z_recv.at[0]).wait()
    out_gain[...] = (gx[2, 0] + gx[2, 1]) * factor

    zgain.wait_send()
    for kind in (0, 1):
        for z in range(NZ):

            @pl.when(owner(kind, z) != dp)
            def _():
                turn(kind, z).wait_send()

        for i in range(6):
            sends[kind][i].wait_send()
    every = pl.ds(0, tokens)
    for t in range(1, 4):
        quarters(0, t, xn_st, xnq, every, 0).wait_send()
        quarters(1, t, dyb_st, dybq, every, 0).wait_send()
        units_of(0, t, dpq, every, 0).wait_send()
        units_of(1, t, hq, every, 0).wait_send()
    for phase in (0, 1):
        for t in range(1, 4):
            gain_send(phase, t).wait_send()

    @pl.when(s < last)
    def _():
        loop(nchunk, lambda c: send_x(c).wait_send())

    @pl.when(s > 0)
    def _():
        loop(nchunk, lambda c: send_dy(c).wait_send())


def results(gain_ref, down_ref, up_ref, out_gain, out_down, out_up):
    for b in range(gain_ref.shape[0]):
        out_gain[:, b * 128 : (b + 1) * 128] = gain_ref[b : b + 1, :]
    out_down[0] = down_ref[...]
    out_up[0] = up_ref[...]


def local(inputs, cotangent, stored, sample_ids, act_exp, grad_exp, gain, down_weight, up_weight):
    micro, spm, seq, width = inputs.shape
    tokens = micro * spm * seq
    units = down_weight.shape[2]
    act_exp = jnp.transpose(act_exp, (0, 1, 4, 2, 3))
    grad_exp = jnp.transpose(grad_exp, (0, 1, 4, 2, 3))
    nchunk = tokens // C
    ndp = lax.axis_size("dp")
    factor = 1.0 / math.sqrt(tokens * ndp)
    hbm = pl.BlockSpec(memory_space=pl.ANY)
    vmem = pl.BlockSpec(memory_space=pltpu.VMEM)
    big = pltpu.VMEM((tokens, width), BF16)
    dma = pltpu.SemaphoreType.DMA
    scratch = [
        big, big, big, big, big,
        pltpu.VMEM((width, units), BF16), pltpu.VMEM((width, units), BF16),
        pltpu.VMEM(stored.shape[1:], BF16),
        big, big,
        pltpu.VMEM(act_exp.shape[1:], jnp.int32), pltpu.VMEM(grad_exp.shape[1:], jnp.int32),
        pltpu.VMEM((1, width), F32),
        pltpu.VMEM((128, tokens), F32),
        pltpu.VMEM((tokens, 128), BF16),
        pltpu.VMEM((tokens, 128), F32),
        pltpu.VMEM((tokens, units), F32),
        pltpu.VMEM((C, width), F32),
        pltpu.VMEM((8, width), F32),
        pltpu.VMEM((2, width // 4, units), F32),
        pltpu.VMEM((units, width), BF16), pltpu.VMEM((units, width), BF16),
        pltpu.VMEM((4, tokens, width // 4), BF16), pltpu.VMEM((4, tokens, width // 4), BF16),
        pltpu.VMEM((4, tokens, units), BF16), pltpu.VMEM((4, tokens, units), BF16),
        pltpu.VMEM((2, NZ, NY, BR, 128), BF16), pltpu.VMEM((2, NZ, NY, BR, 128), BF16),
        pltpu.VMEM((2, 2, NZ, BR, 128), BF16),
        pltpu.VMEM((2, 2, 2, NZ, BR, 128), BF16),
        pltpu.VMEM((2, 2, 2, BR, 128), BF16), pltpu.VMEM((2, 2, 2, BR, 128), BF16),
        pltpu.VMEM((3, 4, width // 128, 128), F32),
        dma((6,)), dma((nchunk,)), dma((nchunk,)), dma((nchunk,)), dma((nchunk,)),
        dma((2, 2, 4)), dma((2, 2, 4, 4)), dma((2, 6)), dma((2, 6)),
        dma((2, 4)), dma((2, 4)), dma((1,)), dma((1,)), dma((2, 2)), dma((2, 2)),
    ]
    outs = pl.pallas_call(
        functools.partial(kernel, factor),
        out_shape=(
            jax.ShapeDtypeStruct((width // 128, 128), F32),
            jax.ShapeDtypeStruct((BR, units), F32),
            jax.ShapeDtypeStruct((BR, units), F32),
        ),
        in_specs=[pl.BlockSpec(memory_space=pltpu.SMEM)] + [hbm] * 8,
        out_specs=(vmem, vmem, vmem),
        scratch_shapes=scratch,
        compiler_params=pltpu.CompilerParams(
            collective_id=0, has_side_effects=True, vmem_limit_bytes=60 * 1024 * 1024
        ),
    )(sample_ids, inputs, cotangent, stored, act_exp, grad_exp, gain, down_weight, up_weight)
    return pl.pallas_call(
        results,
        out_shape=(
            jax.ShapeDtypeStruct((1, width), F32),
            jax.ShapeDtypeStruct((1, BR, units), F32),
            jax.ShapeDtypeStruct((1, BR, units), F32),
        ),
        in_specs=[vmem] * 3,
        out_specs=(vmem, vmem, vmem),
    )(*outs)


def solution(mesh):
    placed = (
        P(None, "dp", None, None),
        P(None, "dp", None, None),
        P(None, "dp", None, None),
        P(None, "dp"),
        P(None, None, "dp", None, None),
        P(None, None, "dp", None, None),
        P("section", None),
        P("section", None, None),
        P("section", None, None),
    )
    return jax.shard_map(
        local,
        mesh=mesh,
        in_specs=placed,
        out_specs=(P("section", None), P("section", "dp", None), P("section", "dp", None)),
        check_vma=False,
    )
```

profile of v0, /device:TPU:8, one launch (start us, length us, event | category | flops | bytes accessed | tf_op | source)
XLA Modules:
  0.0 106.7 jit_solution(15881820088972536552)
XLA Ops:
  0.6 104.2 %shard_map.112 = (f32[52,128]{1,0:T(8,128)}, f32[208,256]{1,0:T(8,128)}, f32[208,256]{1,0:T(8,128)}) custom-call(s32[2,2]{1,0:T(2,128)} %ids_ref.1, bf16[2,2,64,6656]{3,2,1,0:T(8,128)(2,1)} %inputs.1, bf16[2,2,64,6656]{3,2,1,0:T(8,128)(2,1)} %cotangent.1, bf16[3,4,64,6656]{3,2,1,0:T(8,128)(2,1)} %stored.1, s32[3,2,52,2,64]{4,3,2,1,0:T(2,128)} %bitcast.2, ...), custom_call_target="tpu_custom_call" | custom-call | tf_op jit(solution)/shard_map/pallas_call | solution.py:633
  104.8 1.8 %shard_map.113 = (f32[1,6656]{1,0:T(1,128)}, f32[1,208,256]{2,1,0:T(8,128)}, f32[1,208,256]{2,1,0:T(8,128)}) custom-call(f32[52,128]{1,0:T(8,128)} %get-tuple-element.6.gain_ref, f32[208,256]{1,0:T(8,128)} %get-tuple-element.7.down_ref, f32[208,256]{1,0:T(8,128)} %get-tuple-element.8.up_ref), custom_call_target="tpu_custom_call" | custom-call | tf_op jit(solution)/shard_map/pallas_call | solution.py:647
where the time goes:
time: 107 us
  Pallas kernels  106 us (99%)
    pallas_call x1, Pallas kernels, local(): pl.pallas_call(functools.partial(kernel, factor), out_shape=(jax.ShapeDty...  104 us

commit v1 on v0

--- a/solution.py
+++ b/solution.py
@@ -197,16 +197,23 @@
     npeer = npeer + jnp.where(xc != yc, NZ, 0)
     pl.semaphore_wait(barrier, npeer + jnp.where(s > 0, 1, 0) + jnp.where(s < last, 1, 0))
 
-    def send_x(c):
+    half = (ntile + 1) // 2
+    whole = (0, ntile)
+    parts = ((0, half), (half, ntile))
+
+    def span(tiles):
+        return pl.ds(tiles[0] * TW, (tiles[1] - tiles[0]) * TW)
+
+    def send_x(c, tiles=whole):
         return pltpu.make_async_remote_copy(
-            src_ref=xout.at[rows_of(c)], dst_ref=x_st.at[rows_of(c)],
+            src_ref=xout.at[rows_of(c), span(tiles)], dst_ref=x_st.at[rows_of(c), span(tiles)],
             send_sem=xs_sem.at[c], recv_sem=xin_sem.at[c],
             device_id={"section": s + 1}, device_id_type=MESH,
         )
 
-    def send_dy(c):
+    def send_dy(c, tiles=whole):
         return pltpu.make_async_remote_copy(
-            src_ref=dyout.at[rows_of(c)], dst_ref=dyb_st.at[rows_of(c)],
+            src_ref=dyout.at[rows_of(c), span(tiles)], dst_ref=dyb_st.at[rows_of(c), span(tiles)],
             send_sem=ds_sem.at[c], recv_sem=dy_sem.at[c],
             device_id={"section": s - 1}, device_id_type=MESH,
         )
@@ -309,8 +316,9 @@
                 xout[rows, cols] = (base + step).astype(BF16)
                 return carry
 
-            lax.fori_loop(0, ntile, code, 0, unroll=True)
-            send_x(c).start()
+            for tiles in parts:
+                lax.fori_loop(*tiles, code, 0, unroll=True)
+                send_x(c, tiles).start()
 
         exchange(0, xn_st, xnq, c)
         exchange_units(1, hq, c)
@@ -358,8 +366,9 @@
                 dyout[rows, cols] = jnp.clip(grad, -128.0 * scale, 127.0 * scale).astype(BF16)
                 return carry
 
-            lax.fori_loop(0, ntile, second, 0, unroll=True)
-            send_dy(c).start()
+            for tiles in parts:
+                lax.fori_loop(*tiles, second, 0, unroll=True)
+                send_dy(c, tiles).start()
 
             @pl.when(s < last)
             def _():

time: 107 us -> 108 us (level); the launches traced: 107 us -> 106 us
  no operation moved by 1% of the time
where the time goes in v1:
time: 108 us; the launch traced here: 106 us
  Pallas kernels  106 us (98%)
    pallas_call x1, Pallas kernels, local(): pl.pallas_call(functools.partial(kernel, factor), out_shape=(jax.ShapeDty...  104 us

profile of v1, /device:TPU:8, one launch (start us, length us, event | category | flops | bytes accessed | tf_op | source)
XLA Modules:
  0.0 106.4 jit_solution(6828477623697482150)
XLA Ops:
  0.6 103.9 %shard_map.112 = (f32[52,128]{1,0:T(8,128)}, f32[208,256]{1,0:T(8,128)}, f32[208,256]{1,0:T(8,128)}) custom-call(s32[2,2]{1,0:T(2,128)} %ids_ref.1, bf16[2,2,64,6656]{3,2,1,0:T(8,128)(2,1)} %inputs.1, bf16[2,2,64,6656]{3,2,1,0:T(8,128)(2,1)} %cotangent.1, bf16[3,4,64,6656]{3,2,1,0:T(8,128)(2,1)} %stored.1, s32[3,2,52,2,64]{4,3,2,1,0:T(2,128)} %bitcast.2, ...), custom_call_target="tpu_custom_call" | custom-call | tf_op jit(solution)/shard_map/pallas_call | solution.py:642
  104.5 1.8 %shard_map.113 = (f32[1,6656]{1,0:T(1,128)}, f32[1,208,256]{2,1,0:T(8,128)}, f32[1,208,256]{2,1,0:T(8,128)}) custom-call(f32[52,128]{1,0:T(8,128)} %get-tuple-element.6.gain_ref, f32[208,256]{1,0:T(8,128)} %get-tuple-element.7.down_ref, f32[208,256]{1,0:T(8,128)} %get-tuple-element.8.up_ref), custom_call_target="tpu_custom_call" | custom-call | tf_op jit(solution)/shard_map/pallas_call | solution.py:656
